TPU v7x, 256 devices: a whole 4x4x8 slice. The times are simulated.
256 devices in a mesh: row: 64 (over y, x, z_lo), col: 4 (over z_hi, core).
Axes of the slice: x: 4, y: 4, z: 8 (z_hi: 2, z_lo: 4; z = z_hi * 4 + z_lo), core: 2. Of those that a mesh axis runs over, the one named last changes fastest.
Arguments:
- row_feats: bfloat16 [262144, 128], P(('row', 'col')), may hold values from -1.2 to 1.2
- row_probes: bfloat16 [16, 262144], P(None, ('row', 'col')), may hold values from -6 to 6
- col_feats: bfloat16 [4, 128, 8192], P('col', None, 'row'), may hold values from -1.2 to 1.2
- col_probes: bfloat16 [4, 16, 8192], P('col', None, 'row'), may hold values from -6 to 6
- lengthscale: float32 [128], replicated, may hold values from 0.6 to 1.6
- outputscale: float32 [1], replicated, may hold values from 0.08 to 0.3
- tile_ids: int32 [64, 4, 4], P('row', 'col'), may hold values from 0 to 7, as said below
- tile_counts: int32 [64, 4], P('row', 'col'), may hold values from 1 to 4, as said below
Outputs:
- row_result: float32 [16, 262144], P(None, ('row', 'col'))
- col_result: float32 [4, 16, 8192], P('col', None, 'row')
Inputs may be any that keep to these rules, and one draw needn't show every extreme that they name: `tile_ids`: within one device's list the 4 entries are distinct; entries at or past the count are ignored. `tile_counts`: devices of the first row index hold exactly 4 live tiles.
All inputs are finite; a program needn't handle non-finite values.
Results may differ from a plain program's by a relative error of at most 0.014.
Values may be sent and summed in bfloat16 or wider, within the bound.
A program may use at most 64 MiB of HBM per device.

v0:
```python
import jax
import jax.numpy as jnp
from jax import lax
from jax.sharding import PartitionSpec as P

P_SIZE = 16
BLK = 2048
CB = 4


def kernel_block(row_part, row_norm, col_part, col_norm, factor):
    product = jnp.dot(row_part, col_part, preferred_element_type=jnp.float32)
    distance = row_norm[:, None] + col_norm[None, :] - 2.0 * product
    return (factor * jnp.exp(-0.5 * distance)).astype(jnp.bfloat16)


def per_device(
    row_feats, row_probes, col_feats, col_probes, lengthscale, outputscale, tile_ids, tile_counts
):
    row_local = (row_feats.astype(jnp.float32) / lengthscale[None, :]).astype(jnp.bfloat16)
    col_local = (col_feats.astype(jnp.float32) / lengthscale[None, :, None]).astype(jnp.bfloat16)
    row_z, row_vec = (
        lax.all_gather(row_local, "col", axis=0, tiled=True),
        lax.all_gather(row_probes, "col", axis=1, tiled=True),
    )
    row_sq = jnp.sum(jnp.square(row_z.astype(jnp.float32)), axis=1)
    row_span = row_z.shape[0]
    col_span = col_feats.shape[2] * lax.axis_size("row")
    factor = outputscale[0]
    tile_list = tile_ids[0, 0]
    live_count = tile_counts[0, 0]
    row_init = jnp.zeros((P_SIZE, row_span), jnp.float32)
    col_init = jnp.zeros((P_SIZE, col_span), jnp.float32)
    col_z, col_vec = (
        lax.all_gather(col_local, "row", axis=2, tiled=True),
        lax.all_gather(col_probes, "row", axis=2, tiled=True),
    )
    col_z = col_z[0]
    col_vec = col_vec[0]
    col_sq = jnp.sum(jnp.square(col_z.astype(jnp.float32)), axis=0)

    def visit_slot(slot_num, totals):
        row_acc, col_acc = totals
        tile_num = tile_list[slot_num]
        row_start = tile_num // CB * BLK
        col_start = tile_num % CB * BLK
        row_part = lax.dynamic_slice_in_dim(row_z, row_start, BLK, 0)
        row_norm = lax.dynamic_slice_in_dim(row_sq, row_start, BLK, 0)
        row_probe = lax.dynamic_slice_in_dim(row_vec, row_start, BLK, 1)
        col_part = lax.dynamic_slice_in_dim(col_z, col_start, BLK, 1)
        col_norm = lax.dynamic_slice_in_dim(col_sq, col_start, BLK, 0)
        col_probe = lax.dynamic_slice_in_dim(col_vec, col_start, BLK, 1)
        kernel_tile = kernel_block(row_part, row_norm, col_part, col_norm, factor)
        row_sum = lax.dot_general(
            col_probe, kernel_tile, (((1,), (1,)), ((), ())), preferred_element_type=jnp.float32
        )
        col_sum = jnp.dot(row_probe, kernel_tile, preferred_element_type=jnp.float32)
        old_rows = lax.dynamic_slice_in_dim(row_acc, row_start, BLK, 1)
        row_acc = lax.dynamic_update_slice_in_dim(row_acc, old_rows + row_sum, row_start, 1)
        old_cols = lax.dynamic_slice_in_dim(col_acc, col_start, BLK, 1)
        col_acc = lax.dynamic_update_slice_in_dim(col_acc, old_cols + col_sum, col_start, 1)
        return (row_acc, col_acc)

    row_total, col_total = lax.fori_loop(0, live_count, visit_slot, (row_init, col_init))
    row_result = lax.psum_scatter(
        row_total.astype(jnp.bfloat16), "col", scatter_dimension=1, tiled=True
    ).astype(jnp.float32)
    col_result = lax.psum_scatter(col_total[None], "row", scatter_dimension=2, tiled=True)
    return (row_result, col_result)


def solution(mesh):
    placed = (
        P(("row", "col"), None),
        P(None, ("row", "col")),
        P("col", None, "row"),
        P("col", None, "row"),
        P(),
        P(),
        P("row", "col", None),
        P("row", "col"),
    )
    return jax.shard_map(
        per_device,
        mesh=mesh,
        in_specs=placed,
        out_specs=(P(None, ("row", "col")), P("col", None, "row")),
        check_vma=False,
    )
```

profile of v0, /device:TPU:2, one launch (start us, length us, event | category | flops | bytes accessed | tf_op | source)
XLA Modules:
  0.0 780.4 jit_solution(12282329832700381504)
XLA Ops:
  7.2 0.0 all-gather.3.cloned.1.call-start
  7.2 1.7 divide_convert_fusion
  8.9 0.0 all-gather.3.cloned.1.call-update
  8.9 0.0 all-gather.5.cloned.1.call-start
  9.0 1.5 divide_convert_fusion.1
  10.5 0.0 all-gather.5.cloned.1.call-update
  10.5 0.0 reduce-scatter.3.cloned.1.call-start
  10.5 11.0 %all_gather.15 = bf16[16,4096]{1,0:T(8,128)(2,1)S(1)} all-gather(bf16[16,1024]{1,0:T(8,128)(2,1)} %param.11), channel_id=1, replica_groups=mesh['row'=64,'col'=4] {'col'}, dimensions={1}, use_global_device_ids=true | all-gather | bytes 163840 | tf_op jit(solution)/shard_map/all_gather | solution.py:24
  21.6 178.0 %all_gather.12 = bf16[1,16,8192]{2,1,0:T(8,128)(2,1)S(1)} all-gather(bf16[1,16,128]{2,1,0:T(8,128)(2,1)} %param.13), channel_id=1, replica_groups=mesh['row'=64,'col'=4] {'row'}, dimensions={2}, use_global_device_ids=true | all-gather | bytes 266240 | tf_op jit(solution)/shard_map/all_gather | solution.py:36
  199.6 0.0 all-gather.3.cloned.1.call-done
  199.6 1.8 multiply_reduce_fusion.1
  201.4 117.5 %all-gather.5.cloned.1.call-done = bf16[1,128,8192]{2,1,0:T(8,128)(2,1)} async-done(((bf16[1,128,128]{2,1,0:T(8,128)(2,1)}), bf16[1,128,8192]{2,1,0:T(8,128)(2,1)}) %all-gather.5.cloned.1.call-update) | async-done | bytes 2097168 | tf_op jit(solution)/shard_map/all_gather | solution.py:35
  318.9 2.1 multiply_reduce_fusion
  321.1 44.1 %while.14 = (s32[]{:T(128)}, f32[16,4096]{1,0:T(8,128)S(1)}, f32[16,8192]{1,0:T(8,128)S(1)}, s32[]{:T(128)}, s32[4]{0:T(128)}, /*index=5*/bf16[16,8192]{1,0:T(8,...) while((s32[]{:T(128)}, f32[16,4096]{1,0:T(8,128)S(1)}, ...), condition=%wide.region_3.4_spmd, body=%wide.region_2.3_spmd.sunk | while | flops 1367408640 | bytes 26919976 | solution.py:64
  321.7 1.2 dynamic_slice.79
  325.6 6.4 multiply_convert_fusion.2
  332.1 2.3 fusion.25
  334.3 1.2 fusion.26
  336.2 1.2 dynamic_slice.79
  340.1 6.4 multiply_convert_fusion.2
  346.5 2.3 fusion.25
  348.8 1.2 fusion.26
  350.7 1.2 dynamic_slice.79
  354.6 6.4 multiply_convert_fusion.2
  361.0 2.3 fusion.25
  363.3 1.2 fusion.26
  365.2 0.0 copy-start
  365.2 0.7 convert_element_type.36
  365.9 0.0 reduce-scatter.3.cloned.1.call-update
  365.9 0.0 reduce-scatter.5.cloned.1.call-start
  366.0 0.0 copy-done
  366.0 0.5 reduce-scatter.5.cloned.1.call-update
  366.5 46.7 %reduce-scatter.3.cloned.1.call-done = bf16[16,1024]{1,0:T(8,128)(2,1)} async-done(((bf16[16,4096]{1,0:T(8,128)(2,1)}), bf16[16,1024]{1,0:T(8,128)(2,1)}) %reduce-scatter.3.cloned.1.call-update) | async-done | bytes 32784 | tf_op jit(solution)/shard_map/reduce_scatter | solution.py:65
  413.3 1.4 convert_element_type.37
  414.6 359.2 %reduce-scatter.5.cloned.1.call-done = f32[1,16,128]{2,1,0:T(8,128)} async-done(((f32[1,16,8192]{2,1,0:T(8,128)}), f32[1,16,128]{2,1,0:T(8,128)}) %reduce-scatter.5.cloned.1.call-update) | async-done | bytes 8208 | tf_op jit(solution)/shard_map/reduce_scatter | solution.py:68
  (8 shorter events, 0.1 us)
Async XLA Ops:
  7.2 192.4 %all-gather.3.cloned.1.call-start = ((), (), s32[]{:S(2)}) async-start(), calls=%async_computation.2 | async-start | bytes 1310720 | tf_op jit(solution)/shard_map/all_gather | solution.py:23
  8.9 310.0 %all-gather.5.cloned.1.call-start = ((), (), s32[]{:S(2)}) async-start(), calls=%async_computation.3 | async-start | bytes 2129920 | tf_op jit(solution)/shard_map/all_gather | solution.py:35
  10.5 402.8 %reduce-scatter.3.cloned.1.call-start = ((), (), s32[]{:S(2)}) async-start(), calls=%async_computation.4 | async-start | bytes 163840 | tf_op jit(solution)/shard_map/reduce_scatter | solution.py:65
  365.2 0.8 copy-start
  365.9 408.0 %reduce-scatter.5.cloned.1.call-start = ((), (), s32[]{:S(2)}) async-start(), calls=%async_computation.5 | async-start | bytes 532480 | tf_op jit(solution)/shard_map/reduce_scatter | solution.py:68
Sparse Core Ops, SparseCore 0:
  9.8 35.0 all-gather.2
  47.2 271.7 all-gather.4
  366.0 47.1 reduce-scatter.2
  416.3 357.5 reduce-scatter.4
where the time goes:
time: 791 us; the launch traced here: 780 us
  waiting for transfers between devices  524 us (66%)
  blocking collectives  189 us (24%)
  matrix products  29.7 us (4%)
  between operations  13.8 us (2%)
  loops' own time  10.6 us (1%)
  other arithmetic  9.17 us (1%)
    reduce_scatter x1, waiting for transfers between devices, per_device(): lax.psum_scatter(col_total[None], 'row', scatter_dimension=2, tiled=True)  359 us
    all_gather x1, blocking collectives, per_device(): lax.all_gather(col_probes, 'row', axis=2, tiled=True)  178 us
    all_gather x1, waiting for transfers between devices, per_device(): lax.all_gather(col_local, 'row', axis=2, tiled=True)  118 us
    reduce_scatter x1, waiting for transfers between devices, per_device(): lax.psum_scatter(row_total.astype(jnp.bfloat16), 'col', scatter_dimension...  46.7 us
    dot_general x3, matrix products, kernel_block(): product = jnp.dot(row_part, col_part, preferred_element_type=jnp.float32)  19.2 us
  transfers between devices with their start and end apart: 4, of which 3 were waited for; matrix products, arithmetic and copies ran while one was open for 1% of the time, Pallas kernels for 0%

commit v1 on v0

v1 whole, which is shorter than its diff:
```python
import functools
import math

import jax
import jax.numpy as jnp
from jax import lax
from jax.experimental import pallas as pl
from jax.experimental.pallas import tpu as pltpu
from jax.sharding import PartitionSpec as P

D = 128
P_SIZE = 16
N_EXTRA = 16
DEPTH = D + N_EXTRA
PACK = DEPTH + P_SIZE
HALF = PACK // 2
ROWS = 1024
COLS = 128
SLOTS = 4
N_Q = 4
N_Y = 4
N_X = 4
N_Z = 4
CHUNK = N_X * COLS
LOG2E = math.log2(math.e)
F32 = jnp.float32
BF16 = jnp.bfloat16


def split3(value):
    high = value.astype(BF16).astype(F32)
    rest = value - high
    middle = rest.astype(BF16).astype(F32)
    return high, middle, (rest - middle).astype(BF16).astype(F32)


def kernel(
    row_feats, row_probes, col_feats, col_probes, lengthscale, outputscale, tile_ids, tile_counts,
    row_out, col_out,
    row_z, row_aug, row_vec, own, chunk0, chunk1, chunk2, chunk3,
    row_part, col_part, col_sum, row_send, row_recv, s1_recv, s2_send, s2_recv, s3_send, s3_recv,
    rz_ssem, rz_rsem, z_ssem, z_rsem, g_ssem, g_rsem, rr_ssem, rr_rsem, c_ssem, c_rsem, f_ssem, f_rsem,
):
    chunks = (chunk0, chunk1, chunk2, chunk3)
    row, col = lax.axis_index("row"), lax.axis_index("col")
    y, x, z = row // (N_X * N_Z), (row // N_Z) % N_X, row % N_Z
    chip_hi, core = col // 2, col % 2
    mates = (
        chip_hi * 2 + (1 - core),
        (1 - chip_hi) * 2 + core,
        (1 - chip_hi) * 2 + (1 - core),
    )

    def in_col(yy, xx, zz):
        return ((yy * N_X + xx) * N_Z + zz, col)

    def y_peer(step):
        return (y + step) % N_Y

    def x_peer(step):
        return (x + step) % N_X

    def z_peer(step):
        return (z + step) % N_Z

    def remote(src, dst, ssem, rsem, device):
        return pltpu.make_async_remote_copy(
            src_ref=src, dst_ref=dst, send_sem=ssem, recv_sem=rsem,
            device_id=device, device_id_type=pl.DeviceIdType.MESH,
        )

    here = (row, mates[0])
    sends = []

    def send(src, dst, ssem, rsem, device):
        copy = remote(src, dst, ssem, rsem, device)
        copy.start()
        sends.append(copy)

    def received(dst, rsem):
        remote(dst, dst, rsem, rsem, here).wait_recv()

    barrier = pltpu.get_barrier_semaphore()
    greet = [(row, mate) for mate in mates]
    for step in (1, 2, 3):
        greet += [in_col(y_peer(step), x, z), in_col(y, x_peer(step), z), in_col(y, x, z_peer(step))]
    for device in greet:
        pl.semaphore_signal(barrier, inc=1, device_id=device, device_id_type=pl.DeviceIdType.MESH)

    scale = lengthscale[...]
    tall = jnp.transpose(jnp.broadcast_to(scale, (D, D)))
    col_z = (col_feats[...].astype(F32) / tall).astype(BF16)
    own[0:D] = col_z
    half_sq = -0.5 * jnp.sum(jnp.square(col_z.astype(F32)), axis=0, keepdims=True) + jnp.log(outputscale[...])
    high, middle, low = split3(half_sq)
    place = lax.broadcasted_iota(jnp.int32, (N_EXTRA, COLS), 0)
    extra = jnp.where(place < 3, 1.0, 0.0)
    for k, part in enumerate((high, middle, low)):
        extra = jnp.where(place == 3 + k, part, extra)
    own[D:DEPTH] = extra.astype(BF16)
    own[DEPTH:PACK] = col_probes[...]
    row_z[col] = (row_feats[...].astype(F32) / scale).astype(BF16)
    row_vec[col] = row_probes[...]

    pl.semaphore_wait(barrier, len(greet))

    for k in range(N_Z):
        @pl.when(z == k)
        def _():
            for step in (1, 2, 3):
                remote(own, chunks[k].at[y, x], z_ssem.at[step - 1], z_rsem.at[k], in_col(y, x, (k + step) % N_Z)).start()
            chunks[k][y, x] = own[...]
    for step in (1, 2, 3):
        sends.append(remote(own, own, z_ssem.at[step - 1], z_ssem.at[step - 1], here))
    for half in range(2):
        rows = pl.ds(half * (ROWS // 2), ROWS // 2)
        send(row_z.at[col, rows], row_z.at[col, rows], rz_ssem.at[0, half], rz_rsem.at[0, half], (row, mates[1]))
    send(row_vec.at[col], row_vec.at[col], rz_ssem.at[0, 2], rz_rsem.at[0, 2], (row, mates[1]))
    for half in range(2):
        rows = pl.ds(half * (ROWS // 2), ROWS // 2)
        send(row_z.at[col, rows], row_z.at[col, rows], rz_ssem.at[1, half], rz_rsem.at[1, half], (row, mates[0]))
    send(row_vec.at[col], row_vec.at[col], rz_ssem.at[1, 2], rz_rsem.at[1, 2], (row, mates[0]))

    def augment(q):
        zq = row_z[q]
        row_aug[q, :, 0:D] = zq
        sq = -0.5 * jnp.sum(jnp.square(zq.astype(F32)), axis=1, keepdims=True)
        high, middle, low = split3(sq)
        lane = lax.broadcasted_iota(jnp.int32, (ROWS, D), 1)
        value = jnp.where((lane >= 3) & (lane < 6), 1.0, 0.0)
        for k, part in enumerate((high, middle, low)):
            value = jnp.where(lane == k, part, value)
        row_aug[q, :, D:2 * D] = value.astype(BF16)

    def second_stage(k):
        c = chunks[k]
        for step in (1, 2, 3):
            send(c.at[y, x, 0:HALF], c.at[y, x, 0:HALF], g_ssem.at[k, 0, step - 1], g_rsem.at[k, 0, step - 1], in_col(y, x_peer(step), z))
            send(c.at[y, x, HALF:PACK], c.at[y, x, HALF:PACK], g_ssem.at[k, 1, step - 1], g_rsem.at[k, 1, step - 1], in_col(y_peer(step), x, z))

    def third_stage(k):
        c = chunks[k]
        for step in (1, 2, 3):
            received(c.at[y, x_peer(4 - step), 0:HALF], g_rsem.at[k, 0, step - 1])
        for step in (1, 2, 3):
            part = c.at[y, :, 0:HALF]
            send(part, part, g_ssem.at[k, 2, step - 1], g_rsem.at[k, 2, step - 1], in_col(y_peer(step), x, z))
        for step in (1, 2, 3):
            received(c.at[y_peer(4 - step), x, HALF:PACK], g_rsem.at[k, 1, step - 1])
        for step in (1, 2, 3):
            part = c.at[:, x, HALF:PACK]
            send(part, part, g_ssem.at[k, 3, step - 1], g_rsem.at[k, 3, step - 1], in_col(y, x_peer(step), z))

    def chunk_ready(k):
        c = chunks[k]
        for step in (1, 2, 3):
            received(c.at[y_peer(4 - step), :, 0:HALF], g_rsem.at[k, 2, step - 1])
            received(c.at[:, x_peer(4 - step), HALF:PACK], g_rsem.at[k, 3, step - 1])

    augment(col)
    for k in range(N_Z):
        @pl.when(z != k)
        def _():
            received(chunks[k].at[y, x], z_rsem.at[k])
        second_stage(k)
    third_stage(0)

    for half in range(2):
        rows = pl.ds(half * (ROWS // 2), ROWS // 2)
        received(row_z.at[mates[0], rows], rz_rsem.at[1, half])
    received(row_vec.at[mates[0]], rz_rsem.at[1, 2])
    augment(mates[0])
    for half in range(2):
        rows = pl.ds(half * (ROWS // 2), ROWS // 2)
        received(row_z.at[mates[1], rows], rz_rsem.at[0, half])
        send(row_z.at[mates[1], rows], row_z.at[mates[1], rows], rz_ssem.at[2, half], rz_rsem.at[2, half], (row, mates[0]))
    received(row_vec.at[mates[1]], rz_rsem.at[0, 2])
    send(row_vec.at[mates[1]], row_vec.at[mates[1]], rz_ssem.at[2, 2], rz_rsem.at[2, 2], (row, mates[0]))
    augment(mates[1])
    for half in range(2):
        rows = pl.ds(half * (ROWS // 2), ROWS // 2)
        received(row_z.at[mates[2], rows], rz_rsem.at[2, half])
    received(row_vec.at[mates[2]], rz_rsem.at[2, 2])
    augment(mates[2])

    count = tile_counts[0, 0]

    def compute(k):
        def visit(t, carry):
            tile = tile_ids[0, 0, t]
            i, j = (tile // 4) % 2, tile % 4
            alive = jnp.where(t < count, 1.0, 0.0).astype(F32)
            pieces = [chunks[k][j, s] for s in range(N_X)]
            right = jnp.concatenate([piece[0:DEPTH] for piece in pieces], axis=1)
            col_vec = jnp.concatenate([piece[DEPTH:PACK] for piece in pieces], axis=1)
            col_vec = (col_vec.astype(F32) * alive).astype(BF16)
            sums = jnp.zeros((P_SIZE, CHUNK), F32)
            for h in range(2):
                left = row_aug[2 * i + h, :, 0:DEPTH]
                exponent = jnp.dot(left, right, preferred_element_type=F32)
                tile_values = jnp.exp2(exponent * LOG2E).astype(BF16)
                sums += jnp.dot(row_vec[2 * i + h], tile_values, preferred_element_type=F32)
                part = lax.dot_general(
                    col_vec, tile_values, (((1,), (1,)), ((), ())), preferred_element_type=F32
                )
                row_part[t, h] = part if k == 0 else row_part[t, h] + part
            col_part[t] = sums * alive
            return carry

        lax.fori_loop(0, SLOTS, visit, 0)
        for j in range(N_Y):
            total = jnp.zeros((P_SIZE, CHUNK), F32)
            for t in range(SLOTS):
                total += jnp.where(tile_ids[0, 0, t] % 4 == j, 1.0, 0.0) * col_part[t]
            col_sum[k, j] = total

    def reduce_first(k):
        for step in (1, 2, 3):
            send(col_sum.at[k, y_peer(step)], s1_recv.at[k, step - 1], c_ssem.at[k, 0, step - 1], c_rsem.at[k, 0, step - 1], in_col(y_peer(step), x, z))

    def reduce_second(k):
        for step in (1, 2, 3):
            received(s1_recv.at[k, step - 1], c_rsem.at[k, 0, step - 1])
        total = col_sum[k, y] + s1_recv[k, 0] + s1_recv[k, 1] + s1_recv[k, 2]
        for s in range(N_X):
            s2_send[k, s] = total[:, s * COLS:(s + 1) * COLS]
        for step in (1, 2, 3):
            send(s2_send.at[k, x_peer(step)], s2_recv.at[k, step - 1], c_ssem.at[k, 1, step - 1], c_rsem.at[k, 1, step - 1], in_col(y, x_peer(step), z))

    def reduce_third(k):
        for step in (1, 2, 3):
            received(s2_recv.at[k, step - 1], c_rsem.at[k, 1, step - 1])
        s3_send[k] = s2_send[k, x] + s2_recv[k, 0] + s2_recv[k, 1] + s2_recv[k, 2]

    for k in range(N_Z):
        chunk_ready(k)
        if k + 1 < N_Z:
            third_stage(k + 1)
        if k >= 2:
            reduce_second(k - 2)
        compute(k)
        if k < N_Z - 1:
            reduce_first(k)

    for q in range(N_Q):
        total = jnp.zeros((P_SIZE, ROWS), F32)
        for t in range(SLOTS):
            total += jnp.where((tile_ids[0, 0, t] // 4) % 2 == q // 2, 1.0, 0.0) * row_part[t, q % 2]
        row_send[q] = total.astype(BF16)
    for m, mate in enumerate(mates):
        send(row_send.at[mate], row_recv.at[m], rr_ssem.at[m], rr_rsem.at[m], (row, mate))
    reduce_first(N_Z - 1)
    reduce_second(N_Z - 2)
    reduce_third(0)
    reduce_third(1)
    reduce_second(N_Z - 1)
    reduce_third(N_Z - 2)
    reduce_third(N_Z - 1)
    for step in (1, 2, 3):
        send(s3_send.at[z_peer(step)], s3_recv.at[step - 1], f_ssem.at[step - 1], f_rsem.at[step - 1], in_col(y, x, z_peer(step)))
    for m in range(3):
        received(row_recv.at[m], rr_rsem.at[m])
    row_out[...] = (
        row_send[col].astype(F32) + row_recv[0].astype(F32) + row_recv[1].astype(F32) + row_recv[2].astype(F32)
    )
    for step in (1, 2, 3):
        received(s3_recv.at[step - 1], f_rsem.at[step - 1])
    col_out[...] = s3_send[z] + s3_recv[0] + s3_recv[1] + s3_recv[2]
    for copy in sends:
        copy.wait_send()


def per_device(
    row_feats, row_probes, col_feats, col_probes, lengthscale, outputscale, tile_ids, tile_counts
):
    vmem = pl.BlockSpec(memory_space=pltpu.VMEM)
    smem = pl.BlockSpec(memory_space=pltpu.SMEM)
    dma = pltpu.SemaphoreType.DMA
    row_result, col_result = pl.pallas_call(
        kernel,
        out_shape=(
            jax.ShapeDtypeStruct((P_SIZE, ROWS), F32),
            jax.ShapeDtypeStruct((P_SIZE, COLS), F32),
        ),
        in_specs=[vmem] * 6 + [smem] * 2,
        out_specs=(vmem, vmem),
        scratch_shapes=[
            pltpu.VMEM((N_Q, ROWS, D), BF16),
            pltpu.VMEM((N_Q, ROWS, 2 * D), BF16),
            pltpu.VMEM((N_Q, P_SIZE, ROWS), BF16),
            pltpu.VMEM((PACK, COLS), BF16),
            *[pltpu.VMEM((N_Y, N_X, PACK, COLS), BF16)] * N_Z,
            pltpu.VMEM((SLOTS, 2, P_SIZE, ROWS), F32),
            pltpu.VMEM((SLOTS, P_SIZE, CHUNK), F32),
            pltpu.VMEM((N_Z, N_Y, P_SIZE, CHUNK), F32),
            pltpu.VMEM((N_Q, P_SIZE, ROWS), BF16),
            pltpu.VMEM((3, P_SIZE, ROWS), BF16),
            pltpu.VMEM((N_Z, 3, P_SIZE, CHUNK), F32),
            pltpu.VMEM((N_Z, N_X, P_SIZE, COLS), F32),
            pltpu.VMEM((N_Z, 3, P_SIZE, COLS), F32),
            pltpu.VMEM((N_Z, P_SIZE, COLS), F32),
            pltpu.VMEM((3, P_SIZE, COLS), F32),
            dma((3, 3)), dma((3, 3)),
            dma((3,)), dma((N_Z,)),
            dma((N_Z, 4, 3)), dma((N_Z, 4, 3)),
            dma((3,)), dma((3,)),
            dma((N_Z, 2, 3)), dma((N_Z, 2, 3)),
            dma((3,)), dma((3,)),
        ],
        compiler_params=pltpu.CompilerParams(
            collective_id=0, has_side_effects=True, vmem_limit_bytes=56 * 2**20
        ),
    )(
        row_feats, row_probes, col_feats[0], col_probes[0], lengthscale[None, :], outputscale[None, :],
        tile_ids, tile_counts,
    )
    return row_result, col_result[None]


def solution(mesh):
    placed = (
        P(("row", "col"), None),
        P(None, ("row", "col")),
        P("col", None, "row"),
        P("col", None, "row"),
        P(),
        P(),
        P("row", "col", None),
        P("row", "col"),
    )
    return jax.shard_map(
        per_device,
        mesh=mesh,
        in_specs=placed,
        out_specs=(P(None, ("row", "col")), P("col", None, "row")),
        check_vma=False,
    )
```

time: 791 us -> 79.2 us (0.10); the launches traced: 780 us -> 79 us
  waiting for transfers between devices: 524 us -> 0 us
  blocking collectives: 189 us -> 0 us
  Pallas kernels: 0 us -> 75 us
  matrix products: 29.7 us -> 0 us
  between operations: 13.8 us -> 1.94 us
  loops' own time: 10.6 us -> 0 us
  other arithmetic: 9.17 us -> 0 us
    reduce_scatter x2 -> x0, waiting for transfers between devices: 406 us -> none  [the longest x1 359 us: per_device(): lax.psum_scatter(col_total[None], 'row', scatter_dimension=2, tiled=True)]
    all_gather x2 -> x0, blocking collectives: 189 us -> none  [the longest x1 178 us: per_device(): lax.all_gather(col_probes, 'row', axis=2, tiled=True)]
    all_gather x2 -> x0, waiting for transfers between devices: 118 us -> none  [the longest x1 118 us: per_device(): lax.all_gather(col_local, 'row', axis=2, tiled=True)]
    pallas_call x0 -> x1, Pallas kernels: none -> 75 us  [per_device(): pl.pallas_call(kernel, out_shape=(jax.ShapeDtypeStruct((P_SIZE, ROWS), F3...]
    dot_general x9 -> x0, matrix products: 29.7 us -> none  [the longest x3 19.2 us: kernel_block(): product = jnp.dot(row_part, col_part, preferred_element_type=jnp.float32)]
    another operation x1 -> x0, loops' own time: 10.6 us -> none  [per_device(): lax.fori_loop(0, live_count, visit_slot, (row_init, col_init))]
  transfers between devices with their start and end apart: 4 -> 0, of which waited for: 3 -> 0; matrix products, arithmetic and copies ran while one was open for 1% -> 0% of each run, Pallas kernels for 0% -> 0%
where the time goes in v1:
time: 79.2 us; the launch traced here: 79 us
  Pallas kernels  75 us (95%)
  local copies, waits for them, and re-layouts  2.08 us (3%)
  between operations  1.94 us (2%)
    pallas_call x1, Pallas kernels, per_device(): pl.pallas_call(kernel, out_shape=(jax.ShapeDtypeStruct((P_SIZE, ROWS), F3...  75 us
    unnamed x4, local copies, waits for them, and re-layouts  2.08 us

profile of v1, /device:TPU:2, one launch (start us, length us, event | category | flops | bytes accessed | tf_op | source)
XLA Modules:
  0.0 79.0 jit_solution(11836875182422378742)
XLA Ops:
  1.9 75.0 %shard_map.95 = (f32[16,1024]{1,0:T(8,128)}, f32[16,128]{1,0:T(8,128)}) custom-call(bf16[1024,128]{1,0:T(8,128)(2,1)} %row_feats.1, bf16[16,1024]{1,0:T(8,128)(2,1)} %row_probes.1, bf16[128,128]{1,0:T(8,128)(2,1)} %bitcast.6, bf16[16,128]{1,0:T(8,128)(2,1)} %bitcast.8, f32[1,128]{1,0:T(1,128)} %bitcast.9, f32[1,1]{1,0:T(1,128)} %bitcast.5.outputscale, ...), custom_call_target="tpu_custom_call" | custom-call | tf_op jit(solution)/shard_map/pallas_call | solution.py:279
  76.9 0.0 copy-start
  76.9 1.5 %copy.14 = f32[16,1024]{1,0:T(8,128)} copy(f32[16,1024]{1,0:T(8,128)} %get-tuple-element.8) | data formatting | bytes 131072
  78.4 0.0 copy-done
  78.4 0.6 copy.15
Async XLA Ops:
  76.9 1.5 %copy-start = (f32[16,128]{1,0:T(8,128)S(1)}, f32[16,128]{1,0:T(8,128)}, u32[]{:S(2)}) copy-start(f32[16,128]{1,0:T(8,128)} %get-tuple-element.5) | copy-start | bytes 24580

commit v2 on v1

v2 whole, which is shorter than its diff:
```python
import functools
import math

import jax
import jax.numpy as jnp
from jax import lax
from jax.experimental import pallas as pl
from jax.experimental.pallas import tpu as pltpu
from jax.sharding import PartitionSpec as P

D = 128
P_SIZE = 16
N_EXTRA = 16
DEPTH = D + N_EXTRA
PACK = DEPTH + P_SIZE
HALF = PACK // 2
ROWS = 1024
PARTS = (0, 512, 1024)
N_PART = len(PARTS) - 1
COLS = 128
SLOTS = 4
UNROLL = 4
N_Q = 4
N_Y = 4
N_X = 4
N_Z = 4
N_PEER = N_Y * N_X - 1
CHUNK = N_X * COLS
LOG2E = math.log2(math.e)
F32 = jnp.float32
BF16 = jnp.bfloat16


def split3(value):
    high = value.astype(BF16).astype(F32)
    rest = value - high
    middle = rest.astype(BF16).astype(F32)
    return high, middle, (rest - middle).astype(BF16).astype(F32)


def kernel(
    row_feats, row_probes, col_feats, col_probes, lengthscale_in, outputscale_in, tile_ids_in, tile_counts_in,
    row_out, col_out,
    lengthscale, outputscale, tile_ids, tile_counts, feats_in, cols_in, row_z0, row_z1, row_aug0, row_aug1, row_vec0, row_vec1, own, chunk0, chunk1, chunk2, chunk3,
    row_part0, row_part1, row_send0, row_send1, row_recv0, row_recv1, col_part, col_sum, plane_recv, z_send, z_recv,
    in_sem, rz_ssem, rz_rsem, z_ssem, z_rsem, g_ssem, g_rsem, rr_ssem, rr_rsem, c_ssem, c_rsem, f_ssem, f_rsem,
):
    chunks = (chunk0, chunk1, chunk2, chunk3)
    row_z = (row_z0, row_z1)
    row_aug = (row_aug0, row_aug1)
    row_vec = (row_vec0, row_vec1)
    row_part = (row_part0, row_part1)
    row_send = (row_send0, row_send1)
    row_recv = (row_recv0, row_recv1)
    row, col = lax.axis_index("row"), lax.axis_index("col")
    y, x, z = row // (N_X * N_Z), (row // N_Z) % N_X, row % N_Z
    chip_hi, core = col // 2, col % 2
    mates = (
        chip_hi * 2 + (1 - core),
        (1 - chip_hi) * 2 + core,
        (1 - chip_hi) * 2 + (1 - core),
    )

    def in_col(yy, xx, zz):
        return ((yy * N_X + xx) * N_Z + zz, col)

    def y_peer(step):
        return (y + step) % N_Y

    def x_peer(step):
        return (x + step) % N_X

    def z_peer(step):
        return (z + step) % N_Z

    def remote(src, dst, ssem, rsem, device):
        return pltpu.make_async_remote_copy(
            src_ref=src, dst_ref=dst, send_sem=ssem, recv_sem=rsem,
            device_id=device, device_id_type=pl.DeviceIdType.MESH,
        )

    here = (row, mates[0])
    sends = []

    def send(src, dst, ssem, rsem, device):
        copy = remote(src, dst, ssem, rsem, device)
        copy.start()
        sends.append(copy)

    def received(dst, rsem):
        remote(dst, dst, rsem, rsem, here).wait_recv()

    barrier = pltpu.get_barrier_semaphore()
    greet = [(row, mate) for mate in mates]
    greet += [in_col(y, x, z_peer(step)) for step in (1, 2, 3)]
    plane = [(step // N_X, step % N_X) for step in range(1, N_Y * N_X)]
    greet += [in_col(y_peer(dy), x_peer(dx), z) for dy, dx in plane]
    for device in greet:
        pl.semaphore_signal(barrier, inc=1, device_id=device, device_id_type=pl.DeviceIdType.MESH)

    loads = [
        pltpu.make_async_copy(lengthscale_in, lengthscale, in_sem.at[0]),
        pltpu.make_async_copy(outputscale_in, outputscale, in_sem.at[1]),
        pltpu.make_async_copy(col_feats, cols_in, in_sem.at[2]),
        pltpu.make_async_copy(col_probes, own.at[DEPTH:PACK], in_sem.at[3]),
        pltpu.make_async_copy(row_feats, feats_in, in_sem.at[4]),
        pltpu.make_async_copy(tile_ids_in, tile_ids, in_sem.at[5]),
        pltpu.make_async_copy(tile_counts_in, tile_counts, in_sem.at[6]),
    ]
    spans = [pl.ds(start, end - start) for start, end in zip(PARTS, PARTS[1:])]
    for p, span in enumerate(spans):
        loads.append(pltpu.make_async_copy(row_probes.at[:, span], row_vec[p].at[col], in_sem.at[7 + p]))
    for load in loads:
        load.start()
    for load in loads[:3]:
        load.wait()
    scale = lengthscale[...]
    tall = jnp.transpose(jnp.broadcast_to(scale, (D, D)))
    col_z = (cols_in[...].astype(F32) / tall).astype(BF16)
    own[0:D] = col_z
    gain = jnp.log(jnp.full((1, COLS), outputscale[0], F32))
    half_sq = gain - 0.5 * jnp.sum(jnp.square(col_z.astype(F32)), axis=0, keepdims=True)
    high, middle, low = split3(half_sq)
    place = lax.broadcasted_iota(jnp.int32, (N_EXTRA, COLS), 0)
    extra = jnp.where(place < 3, 1.0, 0.0)
    for k, part in enumerate((high, middle, low)):
        extra = jnp.where(place == 3 + k, part, extra)
    own[D:DEPTH] = extra.astype(BF16)
    for load in loads[3:]:
        load.wait()
    chunk0[y, x] = own[...]
    for p, span in enumerate(spans):
        row_z[p][col] = (feats_in[span].astype(F32) / scale).astype(BF16)

    pl.semaphore_wait(barrier, len(greet))

    def second_stage(s):
        c = chunks[s]
        for step in (1, 2, 3):
            send(c.at[y, x, 0:HALF], c.at[y, x, 0:HALF], g_ssem.at[s, 0, step - 1], g_rsem.at[s, 0, step - 1], in_col(y, x_peer(step), z))
            send(c.at[y, x, HALF:PACK], c.at[y, x, HALF:PACK], g_ssem.at[s, 1, step - 1], g_rsem.at[s, 1, step - 1], in_col(y_peer(step), x, z))

    def third_stage(s):
        c = chunks[s]
        for step in (1, 2, 3):
            received(c.at[y, x_peer(4 - step), 0:HALF], g_rsem.at[s, 0, step - 1])
        for step in (1, 2, 3):
            part = c.at[y, :, 0:HALF]
            send(part, part, g_ssem.at[s, 2, step - 1], g_rsem.at[s, 2, step - 1], in_col(y_peer(step), x, z))
        for step in (1, 2, 3):
            received(c.at[y_peer(4 - step), x, HALF:PACK], g_rsem.at[s, 1, step - 1])
        for step in (1, 2, 3):
            part = c.at[:, x, HALF:PACK]
            send(part, part, g_ssem.at[s, 3, step - 1], g_rsem.at[s, 3, step - 1], in_col(y, x_peer(step), z))

    def chunk_ready(s):
        c = chunks[s]
        for step in (1, 2, 3):
            received(c.at[y_peer(4 - step), :, 0:HALF], g_rsem.at[s, 2, step - 1])
            received(c.at[:, x_peer(4 - step), HALF:PACK], g_rsem.at[s, 3, step - 1])

    def send_rows(hop, q, h, mate):
        send(row_z[h].at[q], row_z[h].at[q], rz_ssem.at[hop, h, 0], rz_rsem.at[hop, h, 0], (row, mate))
        send(row_vec[h].at[q], row_vec[h].at[q], rz_ssem.at[hop, h, 1], rz_rsem.at[hop, h, 1], (row, mate))

    def rows_received(hop, q, h):
        received(row_z[h].at[q], rz_rsem.at[hop, h, 0])
        received(row_vec[h].at[q], rz_rsem.at[hop, h, 1])

    def augment(q, h):
        zq = row_z[h][q]
        row_aug[h][q, :, 0:D] = zq
        sq = -0.5 * jnp.sum(jnp.square(zq.astype(F32)), axis=1, keepdims=True)
        high, middle, low = split3(sq)
        lane = lax.broadcasted_iota(jnp.int32, zq.shape, 1)
        value = jnp.where((lane >= 3) & (lane < 6), 1.0, 0.0)
        for k, part in enumerate((high, middle, low)):
            value = jnp.where(lane == k, part, value)
        row_aug[h][q, :, D:2 * D] = value.astype(BF16)

    for step in (1, 2, 3):
        send(own, chunks[4 - step].at[y, x], z_ssem.at[step - 1], z_rsem.at[3 - step], in_col(y, x, z_peer(step)))
    second_stage(0)
    for h in range(N_PART):
        send_rows(1, col, h, mates[0])
    augment(col, 0)
    rows_received(1, mates[0], 0)
    augment(mates[0], 0)
    third_stage(0)
    for s in (1, 2, 3):
        received(chunks[s].at[y, x], z_rsem.at[s - 1])
        second_stage(s)
    send_rows(0, col, 0, mates[1])
    third_stage(1)
    third_stage(2)
    third_stage(3)
    augment(col, 1)
    rows_received(1, mates[0], 1)
    augment(mates[0], 1)
    rows_received(0, mates[1], 0)
    send_rows(2, mates[1], 0, mates[0])
    send_rows(0, col, 1, mates[1])
    augment(mates[1], 0)
    rows_received(2, mates[2], 0)
    augment(mates[2], 0)

    count = tile_counts[0, 0]
    started = set()

    def compute(s, parts):
        def visit(t, carry):
            tile = tile_ids[0, 0, t]
            i, j = (tile // 4) % 2, tile % 4
            alive = jnp.where(t < count, 1.0, 0.0).astype(F32)
            pieces = [chunks[s][j, k] for k in range(N_X)]
            right = jnp.concatenate([piece[0:DEPTH] for piece in pieces], axis=1)
            col_vec = jnp.concatenate([piece[DEPTH:PACK] for piece in pieces], axis=1)
            col_vec = (col_vec.astype(F32) * alive).astype(BF16)
            sums = jnp.zeros((P_SIZE, CHUNK), F32)
            for h in parts:
                left = row_aug[h][pl.ds(2 * i, 2)].reshape(-1, 2 * D)[:, 0:DEPTH]
                vec = jnp.concatenate([row_vec[h][2 * i], row_vec[h][2 * i + 1]], axis=1)
                exponent = jnp.dot(left, right, preferred_element_type=F32)
                tile_values = jnp.exp2(exponent * LOG2E).astype(BF16)
                sums += jnp.dot(vec, tile_values, preferred_element_type=F32)
                part = lax.dot_general(
                    col_vec, tile_values, (((1,), (1,)), ((), ())), preferred_element_type=F32
                )
                row_part[h][t] = row_part[h][t] + part if ("row", h) in started else part
            sums = sums * alive
            col_part[s, t] = col_part[s, t] + sums if ("col", s) in started else sums
            return carry

        lax.fori_loop(0, SLOTS, visit, 0, unroll=UNROLL)
        started.update([("col", s)] + [("row", h) for h in parts])

    def send_cols(s):
        for j in range(N_Y):
            total = jnp.zeros((P_SIZE, CHUNK), F32)
            for t in range(SLOTS):
                total += jnp.where(tile_ids[0, 0, t] % 4 == j, 1.0, 0.0) * col_part[s, t]
            for k in range(N_X):
                col_sum[s, j, k] = total[:, k * COLS:(k + 1) * COLS]
        for d, (dy, dx) in enumerate(plane):
            remote(col_sum.at[s, y_peer(dy), x_peer(dx)], plane_recv.at[s, d], c_ssem.at[s], c_rsem.at[s], in_col(y_peer(dy), x_peer(dx), z)).start()
        sends.append(remote(plane_recv.at[s], plane_recv.at[s], c_ssem.at[s], c_ssem.at[s], here))

    def plane_total(s):
        received(plane_recv.at[s], c_rsem.at[s])
        total = col_sum[s, y, x]
        for d in range(N_PEER):
            total += plane_recv[s, d]
        return total

    def send_plane(s):
        z_send[s - 1] = plane_total(s)
        send(z_send.at[s - 1], z_recv.at[s - 1], f_ssem.at[s - 1], f_rsem.at[s - 1], in_col(y, x, z_peer(s)))

    def send_row_sums(h):
        size = PARTS[h + 1] - PARTS[h]
        for q in range(N_Q):
            total = jnp.zeros((P_SIZE, size), F32)
            for t in range(SLOTS):
                part = row_part[h][t, :, (q % 2) * size:(q % 2 + 1) * size]
                total += jnp.where((tile_ids[0, 0, t] // 4) % 2 == q // 2, 1.0, 0.0) * part
            row_send[h][q] = total.astype(BF16)
        for m in (1, 2, 0):
            send(row_send[h].at[mates[m]], row_recv[h].at[m], rr_ssem.at[h, m], rr_rsem.at[h, m], (row, mates[m]))

    chunk_ready(0)
    compute(0, (0,))
    chunk_ready(1)
    compute(1, (0,))
    rows_received(0, mates[1], 1)
    send_rows(2, mates[1], 1, mates[0])
    augment(mates[1], 1)
    rows_received(2, mates[2], 1)
    augment(mates[2], 1)
    compute(1, (1,))
    send_cols(1)
    chunk_ready(2)
    compute(2, (0, 1,))
    send_cols(2)
    send_plane(1)
    chunk_ready(3)
    compute(3, (0, 1,))
    send_row_sums(0)
    send_cols(3)
    send_plane(2)
    compute(0, (1,))
    send_row_sums(1)
    send_cols(0)
    send_plane(3)
    col_total = plane_total(0)
    for s in (1, 2, 3):
        received(z_recv.at[s - 1], f_rsem.at[s - 1])
        col_total += z_recv[s - 1]
    col_out[...] = col_total
    for h, span in enumerate(spans):
        total = row_send[h][col].astype(F32)
        for m in range(3):
            received(row_recv[h].at[m], rr_rsem.at[h, m])
            total += row_recv[h][m].astype(F32)
        row_out[:, span] = total
    for copy in sends:
        copy.wait_send()


def per_device(
    row_feats, row_probes, col_feats, col_probes, lengthscale, outputscale, tile_ids, tile_counts
):
    vmem = pl.BlockSpec(memory_space=pltpu.VMEM)
    anywhere = pl.BlockSpec(memory_space=pl.ANY)
    dma = pltpu.SemaphoreType.DMA
    sizes = [end - start for start, end in zip(PARTS, PARTS[1:])]
    row_result, col_result = pl.pallas_call(
        kernel,
        out_shape=(
            pltpu.VMEM((P_SIZE, ROWS), F32),
            pltpu.VMEM((P_SIZE, COLS), F32),
        ),
        in_specs=[anywhere] * 8,
        out_specs=(vmem, vmem),
        scratch_shapes=[
            pltpu.VMEM((1, D), F32),
            pltpu.SMEM((1,), F32),
            pltpu.SMEM((1, 1, SLOTS), jnp.int32),
            pltpu.SMEM((1, 1), jnp.int32),
            pltpu.VMEM((ROWS, D), BF16),
            pltpu.VMEM((D, COLS), BF16),
            *[pltpu.VMEM((N_Q, size, D), BF16) for size in sizes],
            *[pltpu.VMEM((N_Q, size, 2 * D), BF16) for size in sizes],
            *[pltpu.VMEM((N_Q, P_SIZE, size), BF16) for size in sizes],
            pltpu.VMEM((PACK, COLS), BF16),
            *[pltpu.VMEM((N_Y, N_X, PACK, COLS), BF16)] * N_Z,
            *[pltpu.VMEM((SLOTS, P_SIZE, 2 * size), F32) for size in sizes],
            *[pltpu.VMEM((N_Q, P_SIZE, size), BF16) for size in sizes],
            *[pltpu.VMEM((3, P_SIZE, size), BF16) for size in sizes],
            pltpu.VMEM((N_Z, SLOTS, P_SIZE, CHUNK), F32),
            pltpu.VMEM((N_Z, N_Y, N_X, P_SIZE, COLS), F32),
            pltpu.VMEM((N_Z, N_PEER, P_SIZE, COLS), F32),
            pltpu.VMEM((3, P_SIZE, COLS), F32),
            pltpu.VMEM((3, P_SIZE, COLS), F32),
            dma((7 + N_PART,)),
            dma((3, N_PART, 2)), dma((3, N_PART, 2)),
            dma((3,)), dma((3,)),
            dma((N_Z, 4, 3)), dma((N_Z, 4, 3)),
            dma((N_PART, 3)), dma((N_PART, 3)),
            dma((N_Z,)), dma((N_Z,)),
            dma((3,)), dma((3,)),
        ],
        compiler_params=pltpu.CompilerParams(
            collective_id=0, has_side_effects=True, vmem_limit_bytes=56 * 2**20
        ),
    )(
        row_feats, row_probes, col_feats[0], col_probes[0], lengthscale[None, :], outputscale,
        tile_ids, tile_counts,
    )
    return row_result, col_result[None]


def solution(mesh):
    placed = (
        P(("row", "col"), None),
        P(None, ("row", "col")),
        P("col", None, "row"),
        P("col", None, "row"),
        P(),
        P(),
        P("row", "col", None),
        P("row", "col"),
    )
    return jax.shard_map(
        per_device,
        mesh=mesh,
        in_specs=placed,
        out_specs=(P(None, ("row", "col")), P("col", None, "row")),
        check_vma=False,
    )
```

time: 79.2 us -> 60.7 us (0.77)
  Pallas kernels: 75 us -> 57.1 us
  local copies, waits for them, and re-layouts: 2.08 us -> 1.23 us
    pallas_call x1, Pallas kernels: 75 us -> 57.1 us  [per_device(): pl.pallas_call(kernel, out_shape=(pltpu.VMEM((P_SIZE, ROWS), F32), pltpu....]
    unnamed x4 -> x2, local copies, waits for them, and re-layouts: 2.08 us -> 1.23 us
where the time goes in v2:
time: 60.7 us; the launch traced here: 60.2 us
  Pallas kernels  57.1 us (94%)
  between operations  1.93 us (3%)
  local copies, waits for them, and re-layouts  1.23 us (2%)
    pallas_call x1, Pallas kernels, per_device(): pl.pallas_call(kernel, out_shape=(pltpu.VMEM((P_SIZE, ROWS), F32), pltpu....  57.1 us
    unnamed x2, local copies, waits for them, and re-layouts  1.23 us

profile of v2, /device:TPU:2, one launch (start us, length us, event | category | flops | bytes accessed | tf_op | source)
XLA Modules:
  0.0 60.2 jit_solution(9877319609359504119)
XLA Ops:
  1.9 57.1 %shard_map.95 = (f32[16,1024]{1,0:T(8,128)S(1)}, f32[16,128]{1,0:T(8,128)S(1)}) custom-call(bf16[1024,128]{1,0:T(8,128)(2,1)} %row_feats.1, bf16[16,1024]{1,0:T(8,128)(2,1)} %row_probes.1, bf16[128,128]{1,0:T(8,128)(2,1)} %bitcast.5, bf16[16,128]{1,0:T(8,128)(2,1)} %bitcast.6, f32[1,128]{1,0:T(1,128)} %bitcast.7, f32[1]{0:T(128)S(6)} %copy.14.outputscale_in, ...), custom_call_target="tpu_custom_call" | custom-call | tf_op jit(solution)/shard_map/pallas_call | solution.py:316
  59.0 0.6 %copy.12 = f32[16,1024]{1,0:T(8,128)} copy(f32[16,1024]{1,0:T(8,128)S(1)} %get-tuple-element.6) | data formatting | bytes 131072
  59.6 0.6 copy.13

commit v3 on v2

--- a/solution.py
+++ b/solution.py
@@ -189,8 +189,9 @@
     third_stage(0)
     for s in (1, 2, 3):
         received(chunks[s].at[y, x], z_rsem.at[s - 1])
+    send_rows(0, col, 0, mates[1])
+    for s in (1, 2, 3):
         second_stage(s)
-    send_rows(0, col, 0, mates[1])
     third_stage(1)
     third_stage(2)
     third_stage(3)
@@ -240,16 +241,16 @@
             for t in range(SLOTS):
                 total += jnp.where(tile_ids[0, 0, t] % 4 == j, 1.0, 0.0) * col_part[s, t]
             for k in range(N_X):
-                col_sum[s, j, k] = total[:, k * COLS:(k + 1) * COLS]
+                col_sum[s, j, k] = total[:, k * COLS:(k + 1) * COLS].astype(BF16)
         for d, (dy, dx) in enumerate(plane):
             remote(col_sum.at[s, y_peer(dy), x_peer(dx)], plane_recv.at[s, d], c_ssem.at[s], c_rsem.at[s], in_col(y_peer(dy), x_peer(dx), z)).start()
         sends.append(remote(plane_recv.at[s], plane_recv.at[s], c_ssem.at[s], c_ssem.at[s], here))
 
     def plane_total(s):
         received(plane_recv.at[s], c_rsem.at[s])
-        total = col_sum[s, y, x]
+        total = col_sum[s, y, x].astype(F32)
         for d in range(N_PEER):
-            total += plane_recv[s, d]
+            total += plane_recv[s, d].astype(F32)
         return total
 
     def send_plane(s):
@@ -337,8 +338,8 @@
             *[pltpu.VMEM((N_Q, P_SIZE, size), BF16) for size in sizes],
             *[pltpu.VMEM((3, P_SIZE, size), BF16) for size in sizes],
             pltpu.VMEM((N_Z, SLOTS, P_SIZE, CHUNK), F32),
-            pltpu.VMEM((N_Z, N_Y, N_X, P_SIZE, COLS), F32),
-            pltpu.VMEM((N_Z, N_PEER, P_SIZE, COLS), F32),
+            pltpu.VMEM((N_Z, N_Y, N_X, P_SIZE, COLS), BF16),
+            pltpu.VMEM((N_Z, N_PEER, P_SIZE, COLS), BF16),
             pltpu.VMEM((3, P_SIZE, COLS), F32),
             pltpu.VMEM((3, P_SIZE, COLS), F32),
             dma((7 + N_PART,)),

time: 60.7 us -> 60.3 us (level)
  no operation moved by 1% of the time
where the time goes in v3:
time: 60.3 us; the launch traced here: 59.9 us
  Pallas kernels  56.8 us (94%)
  between operations  1.93 us (3%)
  local copies, waits for them, and re-layouts  1.23 us (2%)
    pallas_call x1, Pallas kernels, per_device(): pl.pallas_call(kernel, out_shape=(pltpu.VMEM((P_SIZE, ROWS), F32), pltpu....  56.8 us
    unnamed x2, local copies, waits for them, and re-layouts  1.23 us

profile of v3, /device:TPU:2, one launch (start us, length us, event | category | flops | bytes accessed | tf_op | source)
XLA Modules:
  0.0 59.9 jit_solution(3953585517177030693)
XLA Ops:
  1.9 56.8 %shard_map.95 = (f32[16,1024]{1,0:T(8,128)S(1)}, f32[16,128]{1,0:T(8,128)S(1)}) custom-call(bf16[1024,128]{1,0:T(8,128)(2,1)} %row_feats.1, bf16[16,1024]{1,0:T(8,128)(2,1)} %row_probes.1, bf16[128,128]{1,0:T(8,128)(2,1)} %bitcast.5, bf16[16,128]{1,0:T(8,128)(2,1)} %bitcast.6, f32[1,128]{1,0:T(1,128)} %bitcast.7, f32[1]{0:T(128)S(6)} %copy.14.outputscale_in, ...), custom_call_target="tpu_custom_call" | custom-call | tf_op jit(solution)/shard_map/pallas_call | solution.py:317
  58.7 0.6 %copy.12 = f32[16,1024]{1,0:T(8,128)} copy(f32[16,1024]{1,0:T(8,128)S(1)} %get-tuple-element.6) | data formatting | bytes 131072
  59.3 0.6 copy.13
